TPU v7x, 256 devices: a whole 4x4x8 slice. The times are simulated.
256 devices in a mesh: section: 16 (over y_lo, z), expert: 16 (over x, y_hi, core).
Axes of the slice: x: 4, y: 4 (y_hi: 2, y_lo: 2; y = y_hi * 2 + y_lo), z: 8, core: 2. Of those that a mesh axis runs over, the one named last changes fastest.
Arguments:
- activations: bfloat16 [16, 2048, 2048], P('section', 'expert'), may hold values from -6 to 6
- norm_gain: float32 [16, 2048], P('section'), may hold values from 0.1 to 1.9
- w_gate: bfloat16 [16, 2048, 11264], P('section', None, 'expert'), may hold values from -0.125 to 0.125
- w_up: bfloat16 [16, 2048, 11264], P('section', None, 'expert'), may hold values from -0.125 to 0.125
- w_down: bfloat16 [16, 11264, 2048], P('section', 'expert'), may hold values from -0.15625 to 0.15625
- routes: int32 [2, 16, 2048, 2], P(None, 'section', 'expert'), may hold values from 0 to 7, all different within a row; in each aligned block of 128 rows (0 to 127, 128 to 255, ..., all dimensions but the last counted through in order) at most 48 rows name the same one
- gate_levels: int32 [2, 16, 2048, 2], P(None, 'section', 'expert'), may hold values from 1 to 8
Outputs:
- passed_on: bfloat16 [16, 2048, 2048], P('section', 'expert')
Inputs may be any that keep to these rules, and one draw needn't show every extreme that they name: `routes`: the 2 experts of a token differ. Among the 128 tokens of one index of expert in one stop and section, no expert is named by more than 48 tokens, and in every draw some expert is named by exactly 48 of them.
All inputs are finite; a program needn't handle non-finite values.
Results may differ from a plain program's by a relative error of at most 0.0065.
Values may be sent and summed in bfloat16 or wider, within the bound.
No kernel may reach another device: no remote copies, remote signals or barrier semaphores. Data moves between devices by JAX's collectives and lax.ppermute only.
A program may use at most 64 MiB of HBM per device.

v0:
```python
import jax
import jax.numpy as jnp
from jax import lax
from jax.sharding import PartitionSpec as P

STOPS = 2


def passed_along(value, axis, by):
    devices = lax.axis_size(axis)
    return lax.ppermute(value, axis, [(i, (i + by) % devices) for i in range(devices)])


def slot_positions(route_rows, experts):
    onehot = (route_rows[:, :, None] == jnp.arange(experts, dtype=jnp.int32)[None, None, :]).astype(
        jnp.int32
    )
    present = jnp.sum(onehot, axis=1)
    before = jnp.cumsum(present, axis=0) - present
    return jnp.sum(onehot * before[:, None, :], axis=2)


def expert_half(rows, gate_w, up_w, down_w):
    width = rows.shape[2]
    flat = rows.reshape(-1, width)
    gate = jnp.dot(flat, gate_w, preferred_element_type=jnp.float32)
    up = jnp.dot(flat, up_w, preferred_element_type=jnp.float32)
    hidden = (jax.nn.silu(gate) * up).astype(jnp.bfloat16)
    partial_value = jnp.dot(hidden, down_w, preferred_element_type=jnp.float32)
    return partial_value.reshape(rows.shape[0], rows.shape[1], width)


def on_device(activations, norm_gain, w_gate, w_up, w_down, routes, gate_levels):
    devices = lax.axis_size("expert")
    experts = devices // 2
    tok_rows = activations.shape[1]
    width = activations.shape[2]
    top_count = routes.shape[3]
    capacity = min(tok_rows, 3 * tok_rows * top_count // (2 * experts))
    gate_w = w_gate[0]
    up_w = w_up[0]
    down_w = w_down[0]
    gain = norm_gain[0]
    stream = activations
    expert_ids = jnp.arange(experts, dtype=jnp.int32)
    slot_ids = jnp.arange(capacity, dtype=jnp.int32)
    for stop_index in range(STOPS):
        current = stream[0]
        streamf = current.astype(jnp.float32)
        variance = jnp.mean(streamf * streamf, axis=-1, keepdims=True)
        normed = (streamf * lax.rsqrt(variance + 1e-06) * gain).astype(jnp.bfloat16)
        route_rows = routes[stop_index, 0]
        levelf = gate_levels[stop_index, 0].astype(jnp.float32)
        weights = levelf / jnp.sum(levelf, axis=-1, keepdims=True)
        slots = slot_positions(route_rows, experts)
        matches = (route_rows[None, None, :, :] == expert_ids[:, None, None, None]) & (
            slots[None, None, :, :] == slot_ids[None, :, None, None]
        )
        selector = (
            jnp.any(matches, axis=-1).astype(jnp.bfloat16).reshape(experts * capacity, tok_rows)
        )
        dispatched = jnp.dot(selector, normed, preferred_element_type=jnp.float32).astype(
            jnp.bfloat16
        )
        outgoing = jnp.repeat(dispatched.reshape(experts, capacity, width), 2, axis=0)
        partial_value = expert_half(
            lax.all_to_all(outgoing, "expert", split_axis=0, concat_axis=0, tiled=True),
            gate_w,
            up_w,
            down_w,
        )
        returned = lax.all_to_all(partial_value, "expert", split_axis=0, concat_axis=0, tiled=True)
        expert_out = (
            jnp.sum(returned.reshape(experts, 2, capacity, width), axis=1)
            .astype(jnp.bfloat16)
            .reshape(experts * capacity, width)
        )
        index = route_rows * capacity + slots
        picked = jnp.take(expert_out, index, axis=0).astype(jnp.float32)
        branch = jnp.sum(weights[:, :, None] * picked, axis=1)
        updated = (streamf + branch).astype(jnp.bfloat16)
        stream = passed_along(updated[None], "section", 1)
    return stream


def solution(mesh):
    in_specs = (
        P("section", "expert", None),
        P("section", None),
        P("section", None, "expert"),
        P("section", None, "expert"),
        P("section", "expert", None),
        P(None, "section", "expert", None),
        P(None, "section", "expert", None),
    )
    out_specs = P("section", "expert", None)
    return jax.shard_map(
        on_device, mesh=mesh, in_specs=in_specs, out_specs=out_specs, check_vma=False
    )
```

profile of v0, /device:TPU:20, one launch (start us, length us, event | category | flops | bytes accessed | tf_op | source)
XLA Modules:
  0.0 400.6 jit_solution(9239562863259275930)
XLA Ops:
  0.0 0.8 slice_bitcast_fusion
  1.6 1.2 fusion.16
  2.9 1.7 convolution_convert_fusion.1
  4.6 0.4 broadcast_in_dim.10
  5.0 43.1 %all_to_all.20 = bf16[16,48,2048]{2,1,0:T(8,128)(2,1)S(1)} all-to-all(bf16[16,48,2048]{2,1,0:T(8,128)(2,1)S(1)} %bitcast.71), channel_id=1, replica_groups=mesh['section'=16,'expert'=16] {'expert'}, dimensions={0} | all-to-all | bytes 6291456 | tf_op jit(solution)/shard_map/all_to_all | solution.py:67
  48.1 2.5 fusion.10
  50.7 3.6 multiply_convert_fusion.1
  54.3 2.3 copy.39
  56.7 5.8 %fusion.2 = f32[16,48,2048]{2,1,0:T(8,128)} fusion(bf16[16,48,704]{2,1,0:T(8,128)(2,1)} %bitcast.79, bf16[1,704,2048]{2,1,0:T(8,128)(2,1)S(1)} %copy-done), kind=kOutput, calls=%fused_computation.6 | convolution fusion | flops 2214592512 | bytes 10256384 | tf_op jit(solution)/shard_map/dot_general | solution.py:29
  62.5 9.3 %all-to-all-start.1 = ((f32[16,48,2048]{2,1,0:T(8,128)}), f32[16,48,2048]{2,1,0:T(8,128)}, u32[]{:S(2)}, u32[]{:S(2)}) async-start(f32[16,48,2048]{2,1,0:T(8,128)} %fusion.2), calls=%async_computation.1 | async-start | bytes 12582912 | tf_op jit(solution)/shard_map/all_to_all | solution.py:72
  72.4 93.2 %all-to-all-done.1 = f32[16,48,2048]{2,1,0:T(8,128)} async-done(((f32[16,48,2048]{2,1,0:T(8,128)}), f32[16,48,2048]{2,1,0:T(8,128)}, u32[]{:S(2)}, u32[]{:S(2)}) %all-to-all-start.1) | async-done | bytes 6291488 | tf_op jit(solution)/shard_map/all_to_all | solution.py:72
  165.5 5.0 %bitcast_reduce_fusion.1 = bf16[8,48,2048]{2,1,0:T(8,128)(2,1)} fusion(f32[16,48,2048]{2,1,0:T(8,128)} %all-to-all-done.1), kind=kLoop, calls=%fused_computation.3 | loop fusion | flops 786432 | bytes 7864320 | tf_op jit(solution)/shard_map/reduce_sum | solution.py:74
  170.5 5.0 %gather_fusion = bf16[256,2048]{1,0:T(8,128)(2,1)} fusion(bf16[384,2048]{1,0:T(8,128)(2,1)} %bitcast.69, s32[1024]{0:T(1024)S(1)} %pad_clamp_fusion.1), kind=kCustom, calls=%fused_computation.clone | custom fusion | bytes 2098176 | tf_op jit(solution)/shard_map/jit(_take)/gather | solution.py:79
  175.5 2.6 reshape.222
  178.1 5.5 %multiply_reduce_fusion.1 = f32[128,2048]{1,0:T(8,128)S(1)} fusion(bf16[128,2,2048]{2,1,0:T(2,128)(2,1)} %reshape.222, pred[128,2]{1,0:T(8,128)(4,1)S(1)} %copy.38, f32[128,2]{1,0:T(8,128)S(1)} %copy.34), kind=kLoop, calls=%fused_computation.21 | loop fusion | flops 1835008 | bytes 2098432 | tf_op jit(solution)/shard_map/reduce_sum | solution.py:80
  183.7 2.0 collective-permute-start
  185.8 17.0 %collective-permute-done = bf16[1,128,2048]{2,1,0:T(8,128)(2,1)S(1)} collective-permute-done((bf16[1,128,2048]{2,1,0:T(8,128)(2,1)S(1)}, bf16[1,128,2048]{2,1,0:T(8,128)(2,1)S(1)}, u32[]{:S(2)}, u32[]{:S(2)}) %collective-permute-start) | collective-permute-done | bytes 524320 | tf_op jit(solution)/shard_map/ppermute | solution.py:11
  203.0 0.6 convolution_convert_fusion
  203.6 0.4 broadcast_in_dim.14
  204.0 43.1 %all_to_all.21 = bf16[16,48,2048]{2,1,0:T(8,128)(2,1)S(1)} all-to-all(bf16[16,48,2048]{2,1,0:T(8,128)(2,1)S(1)} %bitcast.72), channel_id=1, replica_groups=mesh['section'=16,'expert'=16] {'expert'}, dimensions={0} | all-to-all | bytes 6291456 | tf_op jit(solution)/shard_map/all_to_all | solution.py:67
  247.1 2.5 fusion.8
  249.7 3.6 multiply_convert_fusion
  253.3 2.3 copy.46
  255.7 5.8 %fusion = f32[16,48,2048]{2,1,0:T(8,128)} fusion(bf16[16,48,704]{2,1,0:T(8,128)(2,1)} %bitcast.80, bf16[1,704,2048]{2,1,0:T(8,128)(2,1)S(1)} %copy-done), kind=kOutput, calls=%fused_computation.4 | convolution fusion | flops 2214592512 | bytes 10256384 | tf_op jit(solution)/shard_map/dot_general | solution.py:29
  261.5 9.2 %all-to-all-start.3 = ((f32[16,48,2048]{2,1,0:T(8,128)}), f32[16,48,2048]{2,1,0:T(8,128)}, u32[]{:S(2)}, u32[]{:S(2)}) async-start(f32[16,48,2048]{2,1,0:T(8,128)} %fusion), calls=%async_computation.3 | async-start | bytes 12582912 | tf_op jit(solution)/shard_map/all_to_all | solution.py:72
  271.2 94.3 %all-to-all-done.3 = f32[16,48,2048]{2,1,0:T(8,128)} async-done(((f32[16,48,2048]{2,1,0:T(8,128)}), f32[16,48,2048]{2,1,0:T(8,128)}, u32[]{:S(2)}, u32[]{:S(2)}) %all-to-all-start.3) | async-done | bytes 6291488 | tf_op jit(solution)/shard_map/all_to_all | solution.py:72
  365.4 5.0 %bitcast_reduce_fusion = bf16[8,48,2048]{2,1,0:T(8,128)(2,1)} fusion(f32[16,48,2048]{2,1,0:T(8,128)} %all-to-all-done.3), kind=kLoop, calls=%fused_computation.2 | loop fusion | flops 786432 | bytes 7864320 | tf_op jit(solution)/shard_map/reduce_sum | solution.py:74
  370.4 5.0 %gather_fusion.1 = bf16[256,2048]{1,0:T(8,128)(2,1)} fusion(bf16[384,2048]{1,0:T(8,128)(2,1)} %bitcast.70, s32[1024]{0:T(1024)S(1)} %pad_clamp_fusion), kind=kCustom, calls=%fused_computation.1.clone | custom fusion | bytes 2098176 | tf_op jit(solution)/shard_map/jit(_take)/gather | solution.py:79
  375.4 2.5 reshape.226
  377.9 5.5 %multiply_reduce_fusion = f32[128,2048]{1,0:T(8,128)S(1)} fusion(bf16[128,2,2048]{2,1,0:T(2,128)(2,1)} %reshape.226, pred[128,2]{1,0:T(8,128)(4,1)S(1)} %copy.45, f32[128,2]{1,0:T(8,128)S(1)} %copy.41), kind=kLoop, calls=%fused_computation.20 | loop fusion | flops 1835008 | bytes 2098432 | tf_op jit(solution)/shard_map/reduce_sum | solution.py:80
  383.6 16.2 %collective-permute-done.1 = bf16[1,128,2048]{2,1,0:T(8,128)(2,1)S(1)} collective-permute-done((bf16[1,128,2048]{2,1,0:T(8,128)(2,1)S(1)}, bf16[1,128,2048]{2,1,0:T(8,128)(2,1)S(1)}, u32[]{:S(2)}, u32[]{:S(2)}) %collective-permute-start.1) | collective-permute-done | bytes 524320 | tf_op jit(solution)/shard_map/ppermute | solution.py:11
  399.8 0.8 copy.49
  (53 shorter events, 2.5 us)
Async XLA Ops:
  0.0 56.7 %copy-start = (bf16[1,704,2048]{2,1,0:T(8,128)(2,1)S(1)}, bf16[1,704,2048]{2,1,0:T(8,128)(2,1)}, u32[]{:S(2)}) copy-start(bf16[1,704,2048]{2,1,0:T(8,128)(2,1)} %param.13) | copy-start | bytes 8650756
  5.0 43.1 %copy-start.5 = (bf16[1,2048,704]{1,2,0:T(8,128)(2,1)S(1)}, bf16[1,2048,704]{1,2,0:T(8,128)(2,1)}, u32[]{:S(2)}) copy-start(bf16[1,2048,704]{1,2,0:T(8,128)(2,1)} %param.11) | copy-start | bytes 8650756
  48.1 2.5 copy-start.7
  62.5 9.3 %copy-start.3 = (s32[2,1,128,2]{2,3,1,0:T(2,128)S(1)}, s32[2,1,128,2]{2,3,1,0:T(2,128)}, u32[]{:S(2)}) copy-start(s32[2,1,128,2]{2,3,1,0:T(2,128)} %param.14) | copy-start | bytes 6148
  62.5 9.7 %copy-start.4 = (s32[2,1,128,2]{2,3,1,0:T(2,128)S(1)}, s32[2,1,128,2]{2,3,1,0:T(2,128)}, u32[]{:S(2)}) copy-start(s32[2,1,128,2]{2,3,1,0:T(2,128)} %param.15) | copy-start | bytes 6148
  62.5 103.1 %all-to-all-start.1 = ((f32[16,48,2048]{2,1,0:T(8,128)}), f32[16,48,2048]{2,1,0:T(8,128)}, u32[]{:S(2)}, u32[]{:S(2)}) async-start(f32[16,48,2048]{2,1,0:T(8,128)} %fusion.2), calls=%async_computation.1 | async-start | bytes 12582912 | tf_op jit(solution)/shard_map/all_to_all | solution.py:72
  175.5 8.1 %copy-start.1 = (bf16[1,128,2048]{2,1,0:T(8,128)(2,1)S(1)}, bf16[1,128,2048]{2,1,0:T(8,128)(2,1)}, u32[]{:S(2)}) copy-start(bf16[1,128,2048]{2,1,0:T(8,128)(2,1)} %param.9) | copy-start | bytes 1572868
  178.1 24.9 %copy-start.2 = (f32[1,2048]{1,0:T(1,128)S(1)}, f32[1,2048]{1,0:T(1,128)}, u32[]{:S(2)}) copy-start(f32[1,2048]{1,0:T(1,128)} %param.10) | copy-start | bytes 24580
  183.7 19.0 %collective-permute-start = (bf16[1,128,2048]{2,1,0:T(8,128)(2,1)S(1)}, bf16[1,128,2048]{2,1,0:T(8,128)(2,1)S(1)}, u32[]{:S(2)}, u32[]{:S(2)}) collective-permute-start(bf16[1,128,2048]{2,1,0:T(8,128)(2,1)S(1)} %fusion.19), channel_id=1, source_target_pairs={{0,16},{16,32},{32,48},{48,64},{64,80},{80,96},{96,112},{112,128},... | collective-permute-start | bytes 1572872 | tf_op jit(solution)/shard_map/ppermute | solution.py:11
  204.0 43.1 %copy-start.6 = (bf16[1,2048,704]{1,2,0:T(8,128)(2,1)S(1)}, bf16[1,2048,704]{1,2,0:T(8,128)(2,1)}, u32[]{:S(2)}) copy-start(bf16[1,2048,704]{1,2,0:T(8,128)(2,1)} %param.11) | copy-start | bytes 8650756
  247.1 2.5 copy-start.8
  261.5 104.0 %all-to-all-start.3 = ((f32[16,48,2048]{2,1,0:T(8,128)}), f32[16,48,2048]{2,1,0:T(8,128)}, u32[]{:S(2)}, u32[]{:S(2)}) async-start(f32[16,48,2048]{2,1,0:T(8,128)} %fusion), calls=%async_computation.3 | async-start | bytes 12582912 | tf_op jit(solution)/shard_map/all_to_all | solution.py:72
  383.5 16.3 %collective-permute-start.1 = (bf16[1,128,2048]{2,1,0:T(8,128)(2,1)S(1)}, bf16[1,128,2048]{2,1,0:T(8,128)(2,1)S(1)}, u32[]{:S(2)}, u32[]{:S(2)}) collective-permute-start(bf16[1,128,2048]{2,1,0:T(8,128)(2,1)S(1)} %fusion.23), channel_id=1, source_target_pairs={{0,16},{16,32},{32,48},{48,64},{64,80},{80,96},{96,112},{112,128},... | collective-permute-start | bytes 1572872 | tf_op jit(solution)/shard_map/ppermute | solution.py:11
where the time goes:
time: 401 us
  waiting for transfers between devices  221 us (55%)
  blocking collectives  86.2 us (21%)
  matrix products  26.3 us (7%)
  local copies, waits for them, and re-layouts  23.6 us (6%)
  other arithmetic  23.2 us (6%)
  starting transfers between devices  20.6 us (5%)
    all_to_all x2, waiting for transfers between devices, on_device(): lax.all_to_all(partial_value, 'expert', split_axis=0, concat_axis=0, tile...  187 us
    all_to_all x2, blocking collectives, on_device(): lax.all_to_all(outgoing, 'expert', split_axis=0, concat_axis=0, tiled=True)  86.2 us
    ppermute x2, waiting for transfers between devices, passed_along(): lax.ppermute(value, axis, [(i, (i + by) % devices) for i in range(devices)])  33.2 us
    all_to_all x2, starting transfers between devices, on_device(): lax.all_to_all(partial_value, 'expert', split_axis=0, concat_axis=0, tile...  18.5 us
    gather x4, local copies, waits for them, and re-layouts, on_device(): picked = jnp.take(expert_out, index, axis=0).astype(jnp.float32)  15.1 us
    dot_general x2, matrix products, expert_half(): partial_value = jnp.dot(hidden, down_w, preferred_element_type=jnp.float32)  11.6 us
    reduce_sum x2, other arithmetic, on_device(): branch = jnp.sum(weights[:, :, None] * picked, axis=1)  10.9 us
    reduce_sum x2, other arithmetic, on_device(): jnp.sum(returned.reshape(experts, 2, capacity, width), axis=1)  9.94 us
  transfers between devices with their start and end apart: 4, of which 4 were waited for; matrix products, arithmetic and copies ran while one was open for 0% of the time, Pallas kernels for 0%

commit v1 on v0

v1 whole, which is shorter than its diff:
```python
import functools

import jax
import jax.numpy as jnp
from jax import lax
from jax.experimental import pallas as pl
from jax.experimental.pallas import tpu as pltpu
from jax.sharding import PartitionSpec as P

STOPS = 2
CAPACITY = 48
EPS = 1e-06
CHUNKS = 1
DEPTH = 2
MIB = 1024 * 1024
VMEM = pl.BlockSpec(memory_space=pltpu.VMEM)


def passed_along(value, axis, by):
    devices = lax.axis_size(axis)
    return lax.ppermute(value, axis, [(i, (i + by) % devices) for i in range(devices)])


def sibling(value):
    devices = lax.axis_size("expert")
    return lax.ppermute(value, "expert", [(i, i ^ 1) for i in range(devices)])


def across_chips(value, experts):
    groups = [[2 * chip + core for chip in range(experts)] for core in range(2)]
    shape = (experts, value.shape[0] // experts, value.shape[1])
    moved = lax.all_to_all(
        value.reshape(shape),
        "expert",
        split_axis=0,
        concat_axis=0,
        axis_index_groups=groups,
        tiled=True,
    )
    return moved.reshape(value.shape)


def product(a, b):
    return jnp.dot(a, b, preferred_element_type=jnp.float32)


def product_t(a, b):
    return lax.dot_general(a, b, (((1,), (1,)), ((), ())), preferred_element_type=jnp.float32)


def slot_of_token(routes, experts):
    tokens = routes.shape[1]
    expert_ids = lax.broadcasted_iota(jnp.int32, (experts, tokens), 0)
    named = [routes[k : k + 1, :] == expert_ids for k in range(routes.shape[0])]
    present = functools.reduce(jnp.logical_or, named)
    earlier = lax.broadcasted_iota(jnp.int32, (tokens, tokens), 0) < lax.broadcasted_iota(
        jnp.int32, (tokens, tokens), 1
    )
    ones = jnp.where(present, 1.0, 0.0)
    before = product(ones.astype(jnp.bfloat16), jnp.where(earlier, 1.0, 0.0).astype(jnp.bfloat16))
    before = jnp.where(present, before, -1.0).astype(jnp.int32)
    slot_ids = lax.broadcasted_iota(jnp.int32, (experts, CAPACITY, tokens), 1)
    return named, before[:, None, :] == slot_ids


def dispatch_kernel(stop, routes_ref, stream_ref, rows_ref):
    experts = rows_ref.shape[0] // CAPACITY
    _, hit = slot_of_token(routes_ref[stop], experts)
    chosen = jnp.where(hit, 1.0, 0.0).reshape(rows_ref.shape[0], -1).astype(jnp.bfloat16)
    width = rows_ref.shape[1]
    step = 512
    for n in range(0, width, step):
        cols = slice(n, n + step)
        rows_ref[:, cols] = product(chosen, stream_ref[:, cols]).astype(jnp.bfloat16)


def combine_kernel(stop, routes_ref, levels_ref, back_ref, stream_ref, out_ref):
    slots = back_ref.shape[0]
    experts = slots // CAPACITY
    named, hit = slot_of_token(routes_ref[stop], experts)
    levels = levels_ref[stop].astype(jnp.float32)
    level = sum(jnp.where(at, levels[k : k + 1, :], 0.0) for k, at in enumerate(named))
    leveled = jnp.where(hit, level[:, None, :], 0.0).reshape(slots, -1).T
    total = jnp.sum(leveled, axis=1, keepdims=True)
    leveled = leveled.astype(jnp.bfloat16)
    width = out_ref.shape[1]
    step = 512
    for n in range(0, width, step):
        cols = slice(n, n + step)
        branch = product(leveled, back_ref[:, cols]) / total
        out_ref[:, cols] = (stream_ref[:, cols].astype(jnp.float32) + branch).astype(jnp.bfloat16)


def dispatch(stop, routes, stream, experts):
    tokens, width = stream.shape
    count = experts * CAPACITY
    return pl.pallas_call(
        functools.partial(dispatch_kernel, stop),
        out_shape=jax.ShapeDtypeStruct((count, width), stream.dtype),
        in_specs=[VMEM] * 2,
        out_specs=VMEM,
        compiler_params=pltpu.CompilerParams(vmem_limit_bytes=24 * MIB),
        cost_estimate=pl.CostEstimate(
            flops=2 * count * tokens * width,
            bytes_accessed=2 * (count + tokens) * width,
            transcendentals=0,
        ),
        name="dispatch",
    )(routes, stream)


def combine(stop, routes, levels, back, stream):
    tokens, width = stream.shape
    count = back.shape[0]
    return pl.pallas_call(
        functools.partial(combine_kernel, stop),
        out_shape=jax.ShapeDtypeStruct((tokens, width), stream.dtype),
        in_specs=[VMEM] * 4,
        out_specs=VMEM,
        compiler_params=pltpu.CompilerParams(vmem_limit_bytes=24 * MIB),
        cost_estimate=pl.CostEstimate(
            flops=2 * count * tokens * width,
            bytes_accessed=2 * (count + 2 * tokens) * width,
            transcendentals=0,
        ),
        name="combine",
    )(routes, levels, back, stream)


FIRST = 256


def expert_kernel(*refs):
    parts, (gain_ref, gate0, up0, gate1, up1, down0, down1) = refs[:CHUNKS], refs[CHUNKS : CHUNKS + 7]
    out_ref, hidden_ref = refs[CHUNKS + 7 : CHUNKS + 9]
    gates, ups, downs, normed_ref, sems = refs[CHUNKS + 9 :]
    half, width = gate0.shape
    cut = out_ref.shape[1]
    head, tail = pl.ds(0, FIRST), pl.ds(FIRST, half - FIRST)
    every, cols = pl.ds(0, half), pl.ds(0, cut)
    blocks = [
        [(gate0.at[head], gates.at[0, head]), (up0.at[head], ups.at[0, head])],
        [(gate0.at[tail], gates.at[0, tail]), (up0.at[tail], ups.at[0, tail])],
        [(gate1, gates.at[1]), (up1, ups.at[1])],
        [(down0.at[every, cols], downs.at[0]), (down1.at[every, cols], downs.at[1])],
    ]
    copies = [
        [pltpu.make_async_copy(src, dst, sems.at[b, i]) for i, (src, dst) in enumerate(block)]
        for b, block in enumerate(blocks)
    ]

    def fetch(b):
        for copy in copies[b]:
            copy.start()

    def arrive(b):
        for copy in copies[b]:
            copy.wait()
        if b + DEPTH < len(copies):
            fetch(b + DEPTH)

    for b in range(DEPTH):
        fetch(b)
    rowsf = [part[...].astype(jnp.float32) for part in parts]
    variance = sum(jnp.sum(x * x, axis=-1, keepdims=True) for x in rowsf) / width
    scale = lax.rsqrt(variance + EPS)
    for c, x in enumerate(rowsf):
        at = slice(c * cut, (c + 1) * cut)
        normed_ref[:, at] = (x * scale * gain_ref[:, at]).astype(jnp.bfloat16)

    def hide(side, begin, end):
        gate = product_t(normed_ref[...], gates[side, begin:end])
        up = product_t(normed_ref[...], ups[side, begin:end])
        hidden_ref[side, :, begin:end] = (gate / (1.0 + jnp.exp(-gate)) * up).astype(jnp.bfloat16)

    arrive(0)
    hide(0, 0, FIRST)
    arrive(1)
    hide(0, FIRST, half)
    arrive(2)
    hide(1, 0, half)
    arrive(3)
    down_part(hidden_ref, downs, out_ref)


def down_part(hidden_ref, downs, out_ref):
    for n in range(0, out_ref.shape[1], 512):
        at = slice(n, n + 512)
        out = product(hidden_ref[0], downs[0, :, at]) + product(hidden_ref[1], downs[1, :, at])
        out_ref[:, at] = out.astype(jnp.bfloat16)


def later_kernel(chunk, hidden_ref, down0, down1, out_ref, downs, sems):
    half, cut = downs.shape[1:]
    cols = pl.ds(chunk * cut, cut)
    copies = [
        pltpu.make_async_copy(down.at[pl.ds(0, half), cols], downs.at[i], sems.at[i])
        for i, down in enumerate((down0, down1))
    ]
    for copy in copies:
        copy.start()
    for copy in copies:
        copy.wait()
    down_part(hidden_ref, downs, out_ref)


def expert(parts, gain, gates, ups, downs):
    count, cut = parts[0].shape
    half, width = gates[0].shape
    stored = pl.BlockSpec(memory_space=pl.ANY)
    out, hidden = pl.pallas_call(
        expert_kernel,
        out_shape=[
            jax.ShapeDtypeStruct((count, cut), jnp.bfloat16),
            jax.ShapeDtypeStruct((2, count, half), jnp.bfloat16),
        ],
        in_specs=[VMEM] * (CHUNKS + 1) + [stored] * 6,
        out_specs=[VMEM] * 2,
        scratch_shapes=[
            pltpu.VMEM((2, half, width), jnp.bfloat16),
            pltpu.VMEM((2, half, width), jnp.bfloat16),
            pltpu.VMEM((2, half, cut), jnp.bfloat16),
            pltpu.VMEM((count, width), jnp.bfloat16),
            pltpu.SemaphoreType.DMA((4, 2)),
        ],
        compiler_params=pltpu.CompilerParams(vmem_limit_bytes=56 * MIB),
        cost_estimate=pl.CostEstimate(
            flops=8 * count * width * half + 4 * count * cut * half,
            bytes_accessed=8 * half * width + 4 * half * cut + 4 * count * width,
            transcendentals=2 * count * half,
        ),
        name="expert",
    )(*parts, gain, gates[0], ups[0], gates[1], ups[1], *downs)
    outs = [out]
    for chunk in range(1, CHUNKS):
        outs.append(
            pl.pallas_call(
                functools.partial(later_kernel, chunk),
                out_shape=jax.ShapeDtypeStruct((count, cut), jnp.bfloat16),
                in_specs=[VMEM] + [stored] * 2,
                out_specs=VMEM,
                scratch_shapes=[
                    pltpu.VMEM((2, half, cut), jnp.bfloat16),
                    pltpu.SemaphoreType.DMA((2,)),
                ],
                compiler_params=pltpu.CompilerParams(vmem_limit_bytes=56 * MIB),
                cost_estimate=pl.CostEstimate(
                    flops=4 * count * cut * half,
                    bytes_accessed=4 * half * cut + 2 * count * cut,
                    transcendentals=0,
                ),
                name="later",
            )(hidden, *downs)
        )
    return outs


def on_device(activations, norm_gain, w_gate, w_up, w_down, routes, gate_levels):
    experts = lax.axis_size("expert") // 2
    cut = activations.shape[2] // CHUNKS
    by_token = routes[:, 0].transpose(0, 2, 1)
    levels = gate_levels[:, 0].transpose(0, 2, 1)
    stream = [activations[0, :, c * cut : (c + 1) * cut] for c in range(CHUNKS)]
    gates, ups, downs = [[w[0].T] for w in (w_gate, w_up)] + [[w_down[0]]]
    for s in range(STOPS):
        parts = [across_chips(dispatch(s, by_token, part, experts), experts) for part in stream]
        if s == 0:
            for halves in (gates, ups, downs):
                halves.append(sibling(halves[0]))
        outs = expert(parts, norm_gain, gates, ups, downs)
        stream = [
            passed_along(
                combine(s, by_token, levels, across_chips(out, experts), part), "section", 1
            )
            for out, part in zip(outs, stream)
        ]
    return jnp.concatenate(stream, axis=1)[None]


def solution(mesh):
    in_specs = (
        P("section", "expert", None),
        P("section", None),
        P("section", None, "expert"),
        P("section", None, "expert"),
        P("section", "expert", None),
        P(None, "section", "expert", None),
        P(None, "section", "expert", None),
    )
    out_specs = P("section", "expert", None)
    return jax.shard_map(
        on_device, mesh=mesh, in_specs=in_specs, out_specs=out_specs, check_vma=False
    )
```

time: 401 us -> 163 us (0.41)
  the two profiles are of different devices: /device:TPU:20 before, /device:TPU:2 now
where the time goes in v1:
time: 163 us
  blocking collectives  102 us (63%)
  Pallas kernels  27.6 us (17%)
  waiting for transfers between devices  25 us (15%)
  local copies, waits for them, and re-layouts  5.01 us (3%)
  starting transfers between devices  2.6 us (2%)
    all_to_all x4, blocking collectives, across_chips(): lax.all_to_all(value.reshape(shape), 'expert', split_axis=0, concat_axis=...  102 us
    ppermute x2, waiting for transfers between devices, passed_along(): lax.ppermute(value, axis, [(i, (i + by) % devices) for i in range(devices)])  25 us
    pallas_call x2, Pallas kernels, expert(): pl.pallas_call(expert_kernel, out_shape=[jax.ShapeDtypeStruct((count, cut...  24.9 us
    unnamed x15, local copies, waits for them, and re-layouts  5.01 us
  transfers between devices with their start and end apart: 5, of which 2 were waited for; matrix products, arithmetic and copies ran while one was open for 0% of the time, Pallas kernels for 0%

profile of v1, /device:TPU:2, one launch (start us, length us, event | category | flops | bytes accessed | tf_op | source)
XLA Modules:
  0.0 162.7 jit_solution(1373521064922352095)
XLA Ops:
  0.0 0.0 collective-permute-start
  0.0 0.5 collective-permute-start.1
  0.5 0.0 collective-permute-start.2
  0.5 1.0 copy-done
  1.6 0.7 copy-done.2
  2.2 0.7 dispatch.2
  2.9 28.5 %all_to_all.20 = bf16[8,48,2048]{2,1,0:T(8,128)(2,1)} all-to-all(bf16[8,48,2048]{2,1,0:T(8,128)(2,1)S(1)} %bitcast.25), channel_id=1, replica_groups={{0,2,4,6,8,10,12,14},{1,3,5,7,9,11,13,15},{16,18,20,22,24,26,28,30},{17..., dimensions={0} | all-to-all | bytes 3145728 | tf_op jit(solution)/shard_map/all_to_all | solution.py:32
  31.5 0.0 collective-permute-done.refs_4_
  31.5 0.0 collective-permute-done.1.refs_5_
  31.5 0.0 copy-start.6
  31.5 0.0 collective-permute-done.2.refs_7_
  31.5 1.6 copy-done.5
  33.1 0.9 copy-done.6
  34.0 12.5 %expert.2 = (bf16[384,2048]{1,0:T(8,128)(2,1)}, bf16[2,384,704]{2,1,0:T(8,128)(2,1)}) custom-call(bf16[384,2048]{1,0:T(8,128)(2,1)} %bitcast.35, f32[1,2048]{1,0:T(1,128)} %refs_1_.3, bf16[704,2048]{1,0:T(8,128)(2,1)} %bitcast.41, bf16[704,2048]{1,0:T(8,128)(2,1)} %bitcast.44, bf16[704,2048]{1,0:T(8,128)(2,1)} %copy-done.5, bf16[704,2048]{1,0:T(8,128)(2,1)} %copy-done.6, ...), custom_call_target="tpu_custom_call" | custom-call | flops 6643777536 | bytes 20447232 | tf_op jit(solution)/shard_map/expert/pallas_call | solution.py:211
  46.4 0.0 copy-start.1
  46.4 0.0 copy-start.3
  46.5 0.0 copy-start.4
  46.5 26.1 %all_to_all.21 = bf16[8,48,2048]{2,1,0:T(8,128)(2,1)S(1)} all-to-all(bf16[8,48,2048]{2,1,0:T(8,128)(2,1)} %bitcast.38), channel_id=1, replica_groups={{0,2,4,6,8,10,12,14},{1,3,5,7,9,11,13,15},{16,18,20,22,24,26,28,30},{17..., dimensions={0} | all-to-all | bytes 3145728 | tf_op jit(solution)/shard_map/all_to_all | solution.py:32
  72.6 0.0 copy-done.1
  72.6 0.0 copy-done.3
  72.6 0.0 copy-done.4
  72.6 0.6 combine.2
  73.2 2.0 %collective-permute-start.3 = (bf16[128,2048]{1,0:T(8,128)(2,1)S(1)}, bf16[128,2048]{1,0:T(8,128)(2,1)S(1)}, u32[]{:S(2)}, u32[]{:S(2)}) collective-permute-start(bf16[128,2048]{1,0:T(8,128)(2,1)S(1)} %combine.2), channel_id=1, source_target_pairs={{0,16},{16,32},{32,48},{48,64},{64,80},{80,96},{96,112},{112,128},... | collective-permute-start | bytes 1572872 | tf_op jit(solution)/shard_map/ppermute | solution.py:21
  75.2 13.7 %collective-permute-done.3.stream_ref = bf16[128,2048]{1,0:T(8,128)(2,1)S(1)} collective-permute-done((bf16[128,2048]{1,0:T(8,128)(2,1)S(1)}, bf16[128,2048]{1,0:T(8,128)(2,1)S(1)}, u32[]{:S(2)}, u32[]{:S(2)}) %collective-permute-start.3) | collective-permute-done | bytes 524320 | tf_op jit(solution)/shard_map/ppermute | solution.py:21
  88.9 0.7 dispatch.3
  89.6 24.8 %all_to_all.22 = bf16[8,48,2048]{2,1,0:T(8,128)(2,1)} all-to-all(bf16[8,48,2048]{2,1,0:T(8,128)(2,1)S(1)} %bitcast.26), channel_id=1, replica_groups={{0,2,4,6,8,10,12,14},{1,3,5,7,9,11,13,15},{16,18,20,22,24,26,28,30},{17..., dimensions={0} | all-to-all | bytes 3145728 | tf_op jit(solution)/shard_map/all_to_all | solution.py:32
  114.5 12.5 %expert.3 = (bf16[384,2048]{1,0:T(8,128)(2,1)}, bf16[2,384,704]{2,1,0:T(8,128)(2,1)}) custom-call(bf16[384,2048]{1,0:T(8,128)(2,1)} %bitcast.36, f32[1,2048]{1,0:T(1,128)} %refs_1_.3, bf16[704,2048]{1,0:T(8,128)(2,1)} %bitcast.42, bf16[704,2048]{1,0:T(8,128)(2,1)} %bitcast.45, bf16[704,2048]{1,0:T(8,128)(2,1)} %copy-done.5, bf16[704,2048]{1,0:T(8,128)(2,1)} %copy-done.6, ...), custom_call_target="tpu_custom_call" | custom-call | flops 6643777536 | bytes 20447232 | tf_op jit(solution)/shard_map/expert/pallas_call | solution.py:211
  126.9 22.9 %all_to_all.23 = bf16[8,48,2048]{2,1,0:T(8,128)(2,1)S(1)} all-to-all(bf16[8,48,2048]{2,1,0:T(8,128)(2,1)} %bitcast.37), channel_id=1, replica_groups={{0,2,4,6,8,10,12,14},{1,3,5,7,9,11,13,15},{16,18,20,22,24,26,28,30},{17..., dimensions={0} | all-to-all | bytes 3145728 | tf_op jit(solution)/shard_map/all_to_all | solution.py:32
  149.9 0.6 combine.3
  150.5 0.1 collective-permute-start.4
  150.6 11.3 %collective-permute-done.4 = bf16[128,2048]{1,0:T(8,128)(2,1)S(1)} collective-permute-done((bf16[128,2048]{1,0:T(8,128)(2,1)S(1)}, bf16[128,2048]{1,0:T(8,128)(2,1)S(1)}, u32[]{:S(2)}, u32[]{:S(2)}) %collective-permute-start.4) | collective-permute-done | bytes 524320 | tf_op jit(solution)/shard_map/ppermute | solution.py:21
  161.9 0.8 copy.9
  (3 shorter events, 0.0 us)
Async XLA Ops:
  0.0 31.5 %collective-permute-start = (bf16[704,2048]{1,0:T(8,128)(2,1)}, bf16[704,2048]{1,0:T(8,128)(2,1)S(1)}, u32[]{:S(2)}, u32[]{:S(2)}) collective-permute-start(bf16[704,2048]{1,0:T(8,128)(2,1)} %bitcast.40), channel_id=1, source_target_pairs={{0,1},{1,0},{2,3},{3,2},{4,5},{5,4},{6,7},{7,6},{8,9},{9,8},{10,11... | collective-permute-start | bytes 8650760 | tf_op jit(solution)/shard_map/ppermute | solution.py:26
  0.0 31.5 %collective-permute-start.1 = (bf16[704,2048]{1,0:T(8,128)(2,1)}, bf16[704,2048]{1,0:T(8,128)(2,1)S(1)}, u32[]{:S(2)}, u32[]{:S(2)}) collective-permute-start(bf16[704,2048]{1,0:T(8,128)(2,1)} %bitcast.43), channel_id=1, source_target_pairs={{0,1},{1,0},{2,3},{3,2},{4,5},{5,4},{6,7},{7,6},{8,9},{9,8},{10,11... | collective-permute-start | bytes 8650760 | tf_op jit(solution)/shard_map/ppermute | solution.py:26
  0.5 31.0 %collective-permute-start.2 = (bf16[704,2048]{1,0:T(8,128)(2,1)}, bf16[704,2048]{1,0:T(8,128)(2,1)}, u32[]{:S(2)}, u32[]{:S(2)}) collective-permute-start(bf16[704,2048]{1,0:T(8,128)(2,1)} %bitcast.46), channel_id=1, source_target_pairs={{0,1},{1,0},{2,3},{3,2},{4,5},{5,4},{6,7},{7,6},{8,9},{9,8},{10,11... | collective-permute-start | bytes 8650760 | tf_op jit(solution)/shard_map/ppermute | solution.py:26
  0.5 1.0 copy-start
  1.6 0.7 copy-start.2
  31.5 1.6 copy-start.5
  31.5 2.5 %copy-start.6 = (bf16[704,2048]{1,0:T(8,128)(2,1)}, bf16[704,2048]{1,0:T(8,128)(2,1)S(1)}, u32[]{:S(2)}) copy-start(bf16[704,2048]{1,0:T(8,128)(2,1)S(1)} %collective-permute-done.1.refs_5_) | copy-start | bytes 8650756
  46.4 26.1 %copy-start.1 = (bf16[1,128,2048]{2,1,0:T(8,128)(2,1)S(1)}, bf16[1,128,2048]{2,1,0:T(8,128)(2,1)}, u32[]{:S(2)}) copy-start(bf16[1,128,2048]{2,1,0:T(8,128)(2,1)} %param.7) | copy-start | bytes 1572868
  46.4 26.1 %copy-start.3 = (s32[2,1,128,2]{2,3,1,0:T(2,128)S(1)}, s32[2,1,128,2]{2,3,1,0:T(2,128)}, u32[]{:S(2)}) copy-start(s32[2,1,128,2]{2,3,1,0:T(2,128)} %param.12) | copy-start | bytes 6148
  46.5 26.1 %copy-start.4 = (s32[2,1,128,2]{2,3,1,0:T(2,128)S(1)}, s32[2,1,128,2]{2,3,1,0:T(2,128)}, u32[]{:S(2)}) copy-start(s32[2,1,128,2]{2,3,1,0:T(2,128)} %param.13) | copy-start | bytes 6148
  73.2 15.7 %collective-permute-start.3 = (bf16[128,2048]{1,0:T(8,128)(2,1)S(1)}, bf16[128,2048]{1,0:T(8,128)(2,1)S(1)}, u32[]{:S(2)}, u32[]{:S(2)}) collective-permute-start(bf16[128,2048]{1,0:T(8,128)(2,1)S(1)} %combine.2), channel_id=1, source_target_pairs={{0,16},{16,32},{32,48},{48,64},{64,80},{80,96},{96,112},{112,128},... | collective-permute-start | bytes 1572872 | tf_op jit(solution)/shard_map/ppermute | solution.py:21
  150.5 11.4 %collective-permute-start.4 = (bf16[128,2048]{1,0:T(8,128)(2,1)S(1)}, bf16[128,2048]{1,0:T(8,128)(2,1)S(1)}, u32[]{:S(2)}, u32[]{:S(2)}) collective-permute-start(bf16[128,2048]{1,0:T(8,128)(2,1)S(1)} %combine.3), channel_id=1, source_target_pairs={{0,16},{16,32},{32,48},{48,64},{64,80},{80,96},{96,112},{112,128},... | collective-permute-start | bytes 1572872 | tf_op jit(solution)/shard_map/ppermute | solution.py:21

commit v2 on v1

--- a/solution.py
+++ b/solution.py
@@ -10,7 +10,6 @@
 STOPS = 2
 CAPACITY = 48
 EPS = 1e-06
-CHUNKS = 1
 DEPTH = 2
 MIB = 1024 * 1024
 VMEM = pl.BlockSpec(memory_space=pltpu.VMEM)
@@ -130,19 +129,16 @@
 FIRST = 256
 
 
-def expert_kernel(*refs):
-    parts, (gain_ref, gate0, up0, gate1, up1, down0, down1) = refs[:CHUNKS], refs[CHUNKS : CHUNKS + 7]
-    out_ref, hidden_ref = refs[CHUNKS + 7 : CHUNKS + 9]
-    gates, ups, downs, normed_ref, sems = refs[CHUNKS + 9 :]
-    half, width = gate0.shape
-    cut = out_ref.shape[1]
+def expert_kernel(rows_ref, gain_ref, *refs):
+    gate0, up0, gate1, up1, down0, down1, out_ref = refs[:7]
+    gates, ups, downs, normed_ref, hidden_ref, sems = refs[7:]
+    half = gate0.shape[0]
     head, tail = pl.ds(0, FIRST), pl.ds(FIRST, half - FIRST)
-    every, cols = pl.ds(0, half), pl.ds(0, cut)
     blocks = [
         [(gate0.at[head], gates.at[0, head]), (up0.at[head], ups.at[0, head])],
         [(gate0.at[tail], gates.at[0, tail]), (up0.at[tail], ups.at[0, tail])],
         [(gate1, gates.at[1]), (up1, ups.at[1])],
-        [(down0.at[every, cols], downs.at[0]), (down1.at[every, cols], downs.at[1])],
+        [(down0, downs.at[0]), (down1, downs.at[1])],
     ]
     copies = [
         [pltpu.make_async_copy(src, dst, sems.at[b, i]) for i, (src, dst) in enumerate(block)]
@@ -159,20 +155,16 @@
         if b + DEPTH < len(copies):
             fetch(b + DEPTH)
 
-    for b in range(DEPTH):
-        fetch(b)
-    rowsf = [part[...].astype(jnp.float32) for part in parts]
-    variance = sum(jnp.sum(x * x, axis=-1, keepdims=True) for x in rowsf) / width
-    scale = lax.rsqrt(variance + EPS)
-    for c, x in enumerate(rowsf):
-        at = slice(c * cut, (c + 1) * cut)
-        normed_ref[:, at] = (x * scale * gain_ref[:, at]).astype(jnp.bfloat16)
-
     def hide(side, begin, end):
         gate = product_t(normed_ref[...], gates[side, begin:end])
         up = product_t(normed_ref[...], ups[side, begin:end])
         hidden_ref[side, :, begin:end] = (gate / (1.0 + jnp.exp(-gate)) * up).astype(jnp.bfloat16)
 
+    for b in range(DEPTH):
+        fetch(b)
+    rowsf = rows_ref[...].astype(jnp.float32)
+    variance = jnp.mean(rowsf * rowsf, axis=-1, keepdims=True)
+    normed_ref[...] = (rowsf * lax.rsqrt(variance + EPS) * gain_ref[...]).astype(jnp.bfloat16)
     arrive(0)
     hide(0, 0, FIRST)
     arrive(1)
@@ -180,101 +172,48 @@
     arrive(2)
     hide(1, 0, half)
     arrive(3)
-    down_part(hidden_ref, downs, out_ref)
-
-
-def down_part(hidden_ref, downs, out_ref):
     for n in range(0, out_ref.shape[1], 512):
         at = slice(n, n + 512)
         out = product(hidden_ref[0], downs[0, :, at]) + product(hidden_ref[1], downs[1, :, at])
         out_ref[:, at] = out.astype(jnp.bfloat16)
 
 
-def later_kernel(chunk, hidden_ref, down0, down1, out_ref, downs, sems):
-    half, cut = downs.shape[1:]
-    cols = pl.ds(chunk * cut, cut)
-    copies = [
-        pltpu.make_async_copy(down.at[pl.ds(0, half), cols], downs.at[i], sems.at[i])
-        for i, down in enumerate((down0, down1))
-    ]
-    for copy in copies:
-        copy.start()
-    for copy in copies:
-        copy.wait()
-    down_part(hidden_ref, downs, out_ref)
-
-
-def expert(parts, gain, gates, ups, downs):
-    count, cut = parts[0].shape
-    half, width = gates[0].shape
-    stored = pl.BlockSpec(memory_space=pl.ANY)
-    out, hidden = pl.pallas_call(
+def expert(rows, gain, gates, ups, downs):
+    count, width = rows.shape
+    half = gates[0].shape[0]
+    block = pltpu.VMEM((2, half, width), jnp.bfloat16)
+    return pl.pallas_call(
         expert_kernel,
-        out_shape=[
-            jax.ShapeDtypeStruct((count, cut), jnp.bfloat16),
-            jax.ShapeDtypeStruct((2, count, half), jnp.bfloat16),
-        ],
-        in_specs=[VMEM] * (CHUNKS + 1) + [stored] * 6,
-        out_specs=[VMEM] * 2,
-        scratch_shapes=[
-            pltpu.VMEM((2, half, width), jnp.bfloat16),
-            pltpu.VMEM((2, half, width), jnp.bfloat16),
-            pltpu.VMEM((2, half, cut), jnp.bfloat16),
+        out_shape=jax.ShapeDtypeStruct((count, width), jnp.bfloat16),
+        in_specs=[VMEM] * 2 + [pl.BlockSpec(memory_space=pl.ANY)] * 6,
+        out_specs=VMEM,
+        scratch_shapes=[block] * 3
+        + [
             pltpu.VMEM((count, width), jnp.bfloat16),
+            pltpu.VMEM((2, count, half), jnp.bfloat16),
             pltpu.SemaphoreType.DMA((4, 2)),
         ],
-        compiler_params=pltpu.CompilerParams(vmem_limit_bytes=56 * MIB),
+        compiler_params=pltpu.CompilerParams(vmem_limit_bytes=59 * MIB),
         cost_estimate=pl.CostEstimate(
-            flops=8 * count * width * half + 4 * count * cut * half,
-            bytes_accessed=8 * half * width + 4 * half * cut + 4 * count * width,
+            flops=12 * count * width * half,
+            bytes_accessed=12 * half * width + 4 * count * width,
             transcendentals=2 * count * half,
         ),
         name="expert",
-    )(*parts, gain, gates[0], ups[0], gates[1], ups[1], *downs)
-    outs = [out]
-    for chunk in range(1, CHUNKS):
-        outs.append(
-            pl.pallas_call(
-                functools.partial(later_kernel, chunk),
-                out_shape=jax.ShapeDtypeStruct((count, cut), jnp.bfloat16),
-                in_specs=[VMEM] + [stored] * 2,
-                out_specs=VMEM,
-                scratch_shapes=[
-                    pltpu.VMEM((2, half, cut), jnp.bfloat16),
-                    pltpu.SemaphoreType.DMA((2,)),
-                ],
-                compiler_params=pltpu.CompilerParams(vmem_limit_bytes=56 * MIB),
-                cost_estimate=pl.CostEstimate(
-                    flops=4 * count * cut * half,
-                    bytes_accessed=4 * half * cut + 2 * count * cut,
-                    transcendentals=0,
-                ),
-                name="later",
-            )(hidden, *downs)
-        )
-    return outs
+    )(rows, gain, gates[0], ups[0], gates[1], ups[1], *downs)
 
 
 def on_device(activations, norm_gain, w_gate, w_up, w_down, routes, gate_levels):
     experts = lax.axis_size("expert") // 2
-    cut = activations.shape[2] // CHUNKS
     by_token = routes[:, 0].transpose(0, 2, 1)
     levels = gate_levels[:, 0].transpose(0, 2, 1)
-    stream = [activations[0, :, c * cut : (c + 1) * cut] for c in range(CHUNKS)]
-    gates, ups, downs = [[w[0].T] for w in (w_gate, w_up)] + [[w_down[0]]]
+    stream = activations[0]
+    gates, ups, downs = [[w, sibling(w)] for w in (w_gate[0].T, w_up[0].T, w_down[0])]
     for s in range(STOPS):
-        parts = [across_chips(dispatch(s, by_token, part, experts), experts) for part in stream]
-        if s == 0:
-            for halves in (gates, ups, downs):
-                halves.append(sibling(halves[0]))
-        outs = expert(parts, norm_gain, gates, ups, downs)
-        stream = [
-            passed_along(
-                combine(s, by_token, levels, across_chips(out, experts), part), "section", 1
-            )
-            for out, part in zip(outs, stream)
-        ]
-    return jnp.concatenate(stream, axis=1)[None]
+        rows = across_chips(dispatch(s, by_token, stream, experts), experts)
+        back = across_chips(expert(rows, norm_gain, gates, ups, downs), experts)
+        stream = passed_along(combine(s, by_token, levels, back, stream), "section", 1)
+    return stream[None]
 
 
 def solution(mesh):

time: 163 us -> 162 us (level)
    unnamed x15 -> x13, local copies, waits for them, and re-layouts: 5.01 us -> 4.15 us
where the time goes in v2:
time: 162 us
  blocking collectives  102 us (63%)
  Pallas kernels  27.6 us (17%)
  waiting for transfers between devices  25 us (15%)
  local copies, waits for them, and re-layouts  4.15 us (3%)
  starting transfers between devices  2.59 us (2%)
    all_to_all x4, blocking collectives, across_chips(): lax.all_to_all(value.reshape(shape), 'expert', split_axis=0, concat_axis=...  102 us
    ppermute x2, waiting for transfers between devices, passed_along(): lax.ppermute(value, axis, [(i, (i + by) % devices) for i in range(devices)])  25 us
    pallas_call x2, Pallas kernels, expert(): pl.pallas_call(expert_kernel, out_shape=jax.ShapeDtypeStruct((count, widt...  24.9 us
    unnamed x13, local copies, waits for them, and re-layouts  4.15 us
  transfers between devices with their start and end apart: 5, of which 2 were waited for; matrix products, arithmetic and copies ran while one was open for 0% of the time, Pallas kernels for 0%

profile of v2, /device:TPU:2, one launch (start us, length us, event | category | flops | bytes accessed | tf_op | source)
XLA Modules:
  0.0 161.8 jit_solution(18071347901122557581)
XLA Ops:
  0.0 0.0 collective-permute-start
  0.0 0.5 collective-permute-start.1
  0.5 0.0 collective-permute-start.2
  0.5 0.0 copy-start
  0.5 1.0 copy-done
  1.6 0.0 copy-start.2
  1.6 0.7 copy-done.2
  2.2 0.7 dispatch.2
  2.9 28.5 %all_to_all.20 = bf16[8,48,2048]{2,1,0:T(8,128)(2,1)} all-to-all(bf16[8,48,2048]{2,1,0:T(8,128)(2,1)S(1)} %bitcast.25), channel_id=1, replica_groups={{0,2,4,6,8,10,12,14},{1,3,5,7,9,11,13,15},{16,18,20,22,24,26,28,30},{17..., dimensions={0} | all-to-all | bytes 3145728 | tf_op jit(solution)/shard_map/all_to_all | solution.py:31
  31.5 0.0 collective-permute-done.refs_2_
  31.5 0.0 collective-permute-done.1.refs_3_
  31.5 0.0 collective-permute-done.2.refs_5_
  31.5 1.6 copy-done.5
  33.1 12.5 %expert.2 = bf16[384,2048]{1,0:T(8,128)(2,1)} custom-call(bf16[384,2048]{1,0:T(8,128)(2,1)} %bitcast.35, f32[1,2048]{1,0:T(1,128)} %gain_ref.3, bf16[704,2048]{1,0:T(8,128)(2,1)} %bitcast.41, bf16[704,2048]{1,0:T(8,128)(2,1)} %bitcast.44, bf16[704,2048]{1,0:T(8,128)(2,1)} %copy-done.5, bf16[704,2048]{1,0:T(8,128)(2,1)} %collective-permute-done.1.refs_3_, ...), custom_call_target="tpu_custom_call" | custom-call | flops 6643777536 | bytes 20447232 | tf_op jit(solution)/shard_map/expert/pallas_call | solution.py:185
  45.6 0.0 copy-start.1
  45.6 0.0 copy-start.3
  45.6 0.0 copy-start.4
  45.6 26.1 %all_to_all.21 = bf16[8,48,2048]{2,1,0:T(8,128)(2,1)S(1)} all-to-all(bf16[8,48,2048]{2,1,0:T(8,128)(2,1)} %bitcast.38), channel_id=1, replica_groups={{0,2,4,6,8,10,12,14},{1,3,5,7,9,11,13,15},{16,18,20,22,24,26,28,30},{17..., dimensions={0} | all-to-all | bytes 3145728 | tf_op jit(solution)/shard_map/all_to_all | solution.py:31
  71.7 0.0 copy-done.1
  71.7 0.0 copy-done.3
  71.7 0.0 copy-done.4
  71.7 0.6 combine.2
  72.4 2.0 %collective-permute-start.3 = (bf16[128,2048]{1,0:T(8,128)(2,1)S(1)}, bf16[128,2048]{1,0:T(8,128)(2,1)S(1)}, u32[]{:S(2)}, u32[]{:S(2)}) collective-permute-start(bf16[128,2048]{1,0:T(8,128)(2,1)S(1)} %combine.2), channel_id=1, source_target_pairs={{0,16},{16,32},{32,48},{48,64},{64,80},{80,96},{96,112},{112,128},... | collective-permute-start | bytes 1572872 | tf_op jit(solution)/shard_map/ppermute | solution.py:20
  74.4 13.7 %collective-permute-done.3.stream_ref = bf16[128,2048]{1,0:T(8,128)(2,1)S(1)} collective-permute-done((bf16[128,2048]{1,0:T(8,128)(2,1)S(1)}, bf16[128,2048]{1,0:T(8,128)(2,1)S(1)}, u32[]{:S(2)}, u32[]{:S(2)}) %collective-permute-start.3) | collective-permute-done | bytes 524320 | tf_op jit(solution)/shard_map/ppermute | solution.py:20
  88.1 0.7 dispatch.3
  88.8 24.8 %all_to_all.22 = bf16[8,48,2048]{2,1,0:T(8,128)(2,1)} all-to-all(bf16[8,48,2048]{2,1,0:T(8,128)(2,1)S(1)} %bitcast.26), channel_id=1, replica_groups={{0,2,4,6,8,10,12,14},{1,3,5,7,9,11,13,15},{16,18,20,22,24,26,28,30},{17..., dimensions={0} | all-to-all | bytes 3145728 | tf_op jit(solution)/shard_map/all_to_all | solution.py:31
  113.6 12.5 %expert.3 = bf16[384,2048]{1,0:T(8,128)(2,1)} custom-call(bf16[384,2048]{1,0:T(8,128)(2,1)} %bitcast.36, f32[1,2048]{1,0:T(1,128)} %gain_ref.3, bf16[704,2048]{1,0:T(8,128)(2,1)} %bitcast.42, bf16[704,2048]{1,0:T(8,128)(2,1)} %bitcast.45, bf16[704,2048]{1,0:T(8,128)(2,1)} %copy-done.5, bf16[704,2048]{1,0:T(8,128)(2,1)} %collective-permute-done.1.refs_3_, ...), custom_call_target="tpu_custom_call" | custom-call | flops 6643777536 | bytes 20447232 | tf_op jit(solution)/shard_map/expert/pallas_call | solution.py:185
  126.1 22.9 %all_to_all.23 = bf16[8,48,2048]{2,1,0:T(8,128)(2,1)S(1)} all-to-all(bf16[8,48,2048]{2,1,0:T(8,128)(2,1)} %bitcast.37), channel_id=1, replica_groups={{0,2,4,6,8,10,12,14},{1,3,5,7,9,11,13,15},{16,18,20,22,24,26,28,30},{17..., dimensions={0} | all-to-all | bytes 3145728 | tf_op jit(solution)/shard_map/all_to_all | solution.py:31
  149.0 0.6 combine.3
  149.7 0.1 collective-permute-start.4
  149.8 11.3 %collective-permute-done.4 = bf16[128,2048]{1,0:T(8,128)(2,1)S(1)} collective-permute-done((bf16[128,2048]{1,0:T(8,128)(2,1)S(1)}, bf16[128,2048]{1,0:T(8,128)(2,1)S(1)}, u32[]{:S(2)}, u32[]{:S(2)}) %collective-permute-start.4) | collective-permute-done | bytes 524320 | tf_op jit(solution)/shard_map/ppermute | solution.py:20
  161.0 0.8 copy.9
  (1 shorter events, 0.0 us)
Async XLA Ops:
  0.0 31.5 %collective-permute-start = (bf16[704,2048]{1,0:T(8,128)(2,1)}, bf16[704,2048]{1,0:T(8,128)(2,1)S(1)}, u32[]{:S(2)}, u32[]{:S(2)}) collective-permute-start(bf16[704,2048]{1,0:T(8,128)(2,1)} %bitcast.40), channel_id=1, source_target_pairs={{0,1},{1,0},{2,3},{3,2},{4,5},{5,4},{6,7},{7,6},{8,9},{9,8},{10,11... | collective-permute-start | bytes 8650760 | tf_op jit(solution)/shard_map/ppermute | solution.py:25
  0.0 31.5 %collective-permute-start.1 = (bf16[704,2048]{1,0:T(8,128)(2,1)}, bf16[704,2048]{1,0:T(8,128)(2,1)}, u32[]{:S(2)}, u32[]{:S(2)}) collective-permute-start(bf16[704,2048]{1,0:T(8,128)(2,1)} %bitcast.43), channel_id=1, source_target_pairs={{0,1},{1,0},{2,3},{3,2},{4,5},{5,4},{6,7},{7,6},{8,9},{9,8},{10,11... | collective-permute-start | bytes 8650760 | tf_op jit(solution)/shard_map/ppermute | solution.py:25
  0.5 31.0 %collective-permute-start.2 = (bf16[704,2048]{1,0:T(8,128)(2,1)}, bf16[704,2048]{1,0:T(8,128)(2,1)}, u32[]{:S(2)}, u32[]{:S(2)}) collective-permute-start(bf16[704,2048]{1,0:T(8,128)(2,1)} %bitcast.46), channel_id=1, source_target_pairs={{0,1},{1,0},{2,3},{3,2},{4,5},{5,4},{6,7},{7,6},{8,9},{9,8},{10,11... | collective-permute-start | bytes 8650760 | tf_op jit(solution)/shard_map/ppermute | solution.py:25
  0.5 1.0 copy-start
  1.6 0.7 copy-start.2
  31.5 1.6 %copy-start.5 = (bf16[704,2048]{1,0:T(8,128)(2,1)}, bf16[704,2048]{1,0:T(8,128)(2,1)S(1)}, u32[]{:S(2)}) copy-start(bf16[704,2048]{1,0:T(8,128)(2,1)S(1)} %collective-permute-done.refs_2_) | copy-start | bytes 8650756
  45.6 26.1 %copy-start.1 = (bf16[1,128,2048]{2,1,0:T(8,128)(2,1)S(1)}, bf16[1,128,2048]{2,1,0:T(8,128)(2,1)}, u32[]{:S(2)}) copy-start(bf16[1,128,2048]{2,1,0:T(8,128)(2,1)} %param.7) | copy-start | bytes 1572868
  45.6 26.1 %copy-start.3 = (s32[2,1,128,2]{2,3,1,0:T(2,128)S(1)}, s32[2,1,128,2]{2,3,1,0:T(2,128)}, u32[]{:S(2)}) copy-start(s32[2,1,128,2]{2,3,1,0:T(2,128)} %param.12) | copy-start | bytes 6148
  45.6 26.1 %copy-start.4 = (s32[2,1,128,2]{2,3,1,0:T(2,128)S(1)}, s32[2,1,128,2]{2,3,1,0:T(2,128)}, u32[]{:S(2)}) copy-start(s32[2,1,128,2]{2,3,1,0:T(2,128)} %param.13) | copy-start | bytes 6148
  72.4 15.7 %collective-permute-start.3 = (bf16[128,2048]{1,0:T(8,128)(2,1)S(1)}, bf16[128,2048]{1,0:T(8,128)(2,1)S(1)}, u32[]{:S(2)}, u32[]{:S(2)}) collective-permute-start(bf16[128,2048]{1,0:T(8,128)(2,1)S(1)} %combine.2), channel_id=1, source_target_pairs={{0,16},{16,32},{32,48},{48,64},{64,80},{80,96},{96,112},{112,128},... | collective-permute-start | bytes 1572872 | tf_op jit(solution)/shard_map/ppermute | solution.py:20
  149.7 11.4 %collective-permute-start.4 = (bf16[128,2048]{1,0:T(8,128)(2,1)S(1)}, bf16[128,2048]{1,0:T(8,128)(2,1)S(1)}, u32[]{:S(2)}, u32[]{:S(2)}) collective-permute-start(bf16[128,2048]{1,0:T(8,128)(2,1)S(1)} %combine.3), channel_id=1, source_target_pairs={{0,16},{16,32},{32,48},{48,64},{64,80},{80,96},{96,112},{112,128},... | collective-permute-start | bytes 1572872 | tf_op jit(solution)/shard_map/ppermute | solution.py:20

commit v3 on v2

--- a/solution.py
+++ b/solution.py
@@ -208,9 +208,13 @@
     by_token = routes[:, 0].transpose(0, 2, 1)
     levels = gate_levels[:, 0].transpose(0, 2, 1)
     stream = activations[0]
-    gates, ups, downs = [[w, sibling(w)] for w in (w_gate[0].T, w_up[0].T, w_down[0])]
+    near = (w_gate[0].T, w_up[0].T, w_down[0])
     for s in range(STOPS):
-        rows = across_chips(dispatch(s, by_token, stream, experts), experts)
+        rows = dispatch(s, by_token, stream, experts)
+        if s == 0:
+            rows, *near = lax.optimization_barrier((rows, *near))
+            gates, ups, downs = [[w, sibling(w)] for w in near]
+        rows = across_chips(rows, experts)
         back = across_chips(expert(rows, norm_gain, gates, ups, downs), experts)
         stream = passed_along(combine(s, by_token, levels, back, stream), "section", 1)
     return stream[None]

time: 162 us -> 162 us (level)
  no operation moved by 1% of the time
where the time goes in v3:
time: 162 us
  blocking collectives  103 us (64%)
  Pallas kernels  27.6 us (17%)
  waiting for transfers between devices  24.4 us (15%)
  local copies, waits for them, and re-layouts  4.15 us (3%)
  starting transfers between devices  2.77 us (2%)
    all_to_all x4, blocking collectives, across_chips(): lax.all_to_all(value.reshape(shape), 'expert', split_axis=0, concat_axis=...  103 us
    pallas_call x2, Pallas kernels, expert(): pl.pallas_call(expert_kernel, out_shape=jax.ShapeDtypeStruct((count, widt...  24.9 us
    ppermute x2, waiting for transfers between devices, passed_along(): lax.ppermute(value, axis, [(i, (i + by) % devices) for i in range(devices)])  24.4 us
    unnamed x13, local copies, waits for them, and re-layouts  4.15 us
  transfers between devices with their start and end apart: 5, of which 2 were waited for; matrix products, arithmetic and copies ran while one was open for 0% of the time, Pallas kernels for 0%

profile of v3, /device:TPU:2, one launch (start us, length us, event | category | flops | bytes accessed | tf_op | source)
XLA Modules:
  0.0 161.7 jit_solution(9900450971077965403)
XLA Ops:
  0.0 0.0 copy-start
  0.0 1.0 copy-done
  1.0 0.0 copy-start.2
  1.0 0.7 copy-done.2
  1.7 0.7 dispatch.2
  2.4 0.1 collective-permute-start
  2.5 0.5 collective-permute-start.1
  3.0 0.1 collective-permute-start.2
  3.1 28.5 %all_to_all.20 = bf16[8,48,2048]{2,1,0:T(8,128)(2,1)} all-to-all(bf16[8,48,2048]{2,1,0:T(8,128)(2,1)S(1)} %bitcast.23), channel_id=1, replica_groups={{0,2,4,6,8,10,12,14},{1,3,5,7,9,11,13,15},{16,18,20,22,24,26,28,30},{17..., dimensions={0} | all-to-all | bytes 3145728 | tf_op jit(solution)/shard_map/all_to_all | solution.py:31
  31.6 0.0 collective-permute-done.refs_2_
  31.6 0.0 collective-permute-done.1.refs_3_
  31.6 0.0 collective-permute-done.2.refs_5_
  31.6 1.6 copy-done.5
  33.2 12.5 %expert.2 = bf16[384,2048]{1,0:T(8,128)(2,1)} custom-call(bf16[384,2048]{1,0:T(8,128)(2,1)} %bitcast.35, f32[1,2048]{1,0:T(1,128)} %gain_ref.3, bf16[704,2048]{1,0:T(8,128)(2,1)} %bitcast.41, bf16[704,2048]{1,0:T(8,128)(2,1)} %bitcast.44, bf16[704,2048]{1,0:T(8,128)(2,1)} %copy-done.5, bf16[704,2048]{1,0:T(8,128)(2,1)} %collective-permute-done.1.refs_3_, ...), custom_call_target="tpu_custom_call" | custom-call | flops 6643777536 | bytes 20447232 | tf_op jit(solution)/shard_map/expert/pallas_call | solution.py:185
  45.7 0.0 copy-start.1
  45.7 0.0 copy-start.3
  45.7 0.0 copy-start.4
  45.7 25.9 %all_to_all.21 = bf16[8,48,2048]{2,1,0:T(8,128)(2,1)S(1)} all-to-all(bf16[8,48,2048]{2,1,0:T(8,128)(2,1)} %bitcast.38), channel_id=1, replica_groups={{0,2,4,6,8,10,12,14},{1,3,5,7,9,11,13,15},{16,18,20,22,24,26,28,30},{17..., dimensions={0} | all-to-all | bytes 3145728 | tf_op jit(solution)/shard_map/all_to_all | solution.py:31
  71.6 0.0 copy-done.1
  71.6 0.0 copy-done.3
  71.6 0.0 copy-done.4
  71.6 0.6 combine.2
  72.3 2.0 %collective-permute-start.3 = (bf16[128,2048]{1,0:T(8,128)(2,1)S(1)}, bf16[128,2048]{1,0:T(8,128)(2,1)S(1)}, u32[]{:S(2)}, u32[]{:S(2)}) collective-permute-start(bf16[128,2048]{1,0:T(8,128)(2,1)S(1)} %combine.2), channel_id=1, source_target_pairs={{0,16},{16,32},{32,48},{48,64},{64,80},{80,96},{96,112},{112,128},... | collective-permute-start | bytes 1572872 | tf_op jit(solution)/shard_map/ppermute | solution.py:20
  74.3 13.1 %collective-permute-done.3.stream_ref = bf16[128,2048]{1,0:T(8,128)(2,1)S(1)} collective-permute-done((bf16[128,2048]{1,0:T(8,128)(2,1)S(1)}, bf16[128,2048]{1,0:T(8,128)(2,1)S(1)}, u32[]{:S(2)}, u32[]{:S(2)}) %collective-permute-start.3) | collective-permute-done | bytes 524320 | tf_op jit(solution)/shard_map/ppermute | solution.py:20
  87.4 0.7 dispatch.3
  88.1 25.3 %all_to_all.22 = bf16[8,48,2048]{2,1,0:T(8,128)(2,1)} all-to-all(bf16[8,48,2048]{2,1,0:T(8,128)(2,1)S(1)} %bitcast.26), channel_id=1, replica_groups={{0,2,4,6,8,10,12,14},{1,3,5,7,9,11,13,15},{16,18,20,22,24,26,28,30},{17..., dimensions={0} | all-to-all | bytes 3145728 | tf_op jit(solution)/shard_map/all_to_all | solution.py:31
  113.4 12.5 %expert.3 = bf16[384,2048]{1,0:T(8,128)(2,1)} custom-call(bf16[384,2048]{1,0:T(8,128)(2,1)} %bitcast.36, f32[1,2048]{1,0:T(1,128)} %gain_ref.3, bf16[704,2048]{1,0:T(8,128)(2,1)} %bitcast.42, bf16[704,2048]{1,0:T(8,128)(2,1)} %bitcast.45, bf16[704,2048]{1,0:T(8,128)(2,1)} %copy-done.5, bf16[704,2048]{1,0:T(8,128)(2,1)} %collective-permute-done.1.refs_3_, ...), custom_call_target="tpu_custom_call" | custom-call | flops 6643777536 | bytes 20447232 | tf_op jit(solution)/shard_map/expert/pallas_call | solution.py:185
  125.8 23.1 %all_to_all.23 = bf16[8,48,2048]{2,1,0:T(8,128)(2,1)S(1)} all-to-all(bf16[8,48,2048]{2,1,0:T(8,128)(2,1)} %bitcast.37), channel_id=1, replica_groups={{0,2,4,6,8,10,12,14},{1,3,5,7,9,11,13,15},{16,18,20,22,24,26,28,30},{17..., dimensions={0} | all-to-all | bytes 3145728 | tf_op jit(solution)/shard_map/all_to_all | solution.py:31
  148.9 0.6 combine.3
  149.6 0.1 collective-permute-start.4
  149.6 11.3 %collective-permute-done.4 = bf16[128,2048]{1,0:T(8,128)(2,1)S(1)} collective-permute-done((bf16[128,2048]{1,0:T(8,128)(2,1)S(1)}, bf16[128,2048]{1,0:T(8,128)(2,1)S(1)}, u32[]{:S(2)}, u32[]{:S(2)}) %collective-permute-start.4) | collective-permute-done | bytes 524320 | tf_op jit(solution)/shard_map/ppermute | solution.py:20
  160.9 0.8 copy.9
  (1 shorter events, 0.0 us)
Async XLA Ops:
  0.0 1.0 copy-start
  1.0 0.7 copy-start.2
  2.4 29.2 %collective-permute-start = (bf16[704,2048]{1,0:T(8,128)(2,1)}, bf16[704,2048]{1,0:T(8,128)(2,1)S(1)}, u32[]{:S(2)}, u32[]{:S(2)}) collective-permute-start(bf16[704,2048]{1,0:T(8,128)(2,1)} %bitcast.40), channel_id=1, source_target_pairs={{0,1},{1,0},{2,3},{3,2},{4,5},{5,4},{6,7},{7,6},{8,9},{9,8},{10,11... | collective-permute-start | bytes 8650760 | tf_op jit(solution)/shard_map/ppermute | solution.py:25
  2.5 29.1 %collective-permute-start.1 = (bf16[704,2048]{1,0:T(8,128)(2,1)}, bf16[704,2048]{1,0:T(8,128)(2,1)}, u32[]{:S(2)}, u32[]{:S(2)}) collective-permute-start(bf16[704,2048]{1,0:T(8,128)(2,1)} %bitcast.43), channel_id=1, source_target_pairs={{0,1},{1,0},{2,3},{3,2},{4,5},{5,4},{6,7},{7,6},{8,9},{9,8},{10,11... | collective-permute-start | bytes 8650760 | tf_op jit(solution)/shard_map/ppermute | solution.py:25
  3.0 28.6 %collective-permute-start.2 = (bf16[704,2048]{1,0:T(8,128)(2,1)}, bf16[704,2048]{1,0:T(8,128)(2,1)}, u32[]{:S(2)}, u32[]{:S(2)}) collective-permute-start(bf16[704,2048]{1,0:T(8,128)(2,1)} %bitcast.46), channel_id=1, source_target_pairs={{0,1},{1,0},{2,3},{3,2},{4,5},{5,4},{6,7},{7,6},{8,9},{9,8},{10,11... | collective-permute-start | bytes 8650760 | tf_op jit(solution)/shard_map/ppermute | solution.py:25
  31.6 1.6 %copy-start.5 = (bf16[704,2048]{1,0:T(8,128)(2,1)}, bf16[704,2048]{1,0:T(8,128)(2,1)S(1)}, u32[]{:S(2)}) copy-start(bf16[704,2048]{1,0:T(8,128)(2,1)S(1)} %collective-permute-done.refs_2_) | copy-start | bytes 8650756
  45.7 25.9 %copy-start.1 = (bf16[1,128,2048]{2,1,0:T(8,128)(2,1)S(1)}, bf16[1,128,2048]{2,1,0:T(8,128)(2,1)}, u32[]{:S(2)}) copy-start(bf16[1,128,2048]{2,1,0:T(8,128)(2,1)} %param.7) | copy-start | bytes 1572868
  45.7 25.9 %copy-start.3 = (s32[2,1,128,2]{2,3,1,0:T(2,128)S(1)}, s32[2,1,128,2]{2,3,1,0:T(2,128)}, u32[]{:S(2)}) copy-start(s32[2,1,128,2]{2,3,1,0:T(2,128)} %param.12) | copy-start | bytes 6148
  45.7 25.9 %copy-start.4 = (s32[2,1,128,2]{2,3,1,0:T(2,128)S(1)}, s32[2,1,128,2]{2,3,1,0:T(2,128)}, u32[]{:S(2)}) copy-start(s32[2,1,128,2]{2,3,1,0:T(2,128)} %param.13) | copy-start | bytes 6148
  72.3 15.1 %collective-permute-start.3 = (bf16[128,2048]{1,0:T(8,128)(2,1)S(1)}, bf16[128,2048]{1,0:T(8,128)(2,1)S(1)}, u32[]{:S(2)}, u32[]{:S(2)}) collective-permute-start(bf16[128,2048]{1,0:T(8,128)(2,1)S(1)} %combine.2), channel_id=1, source_target_pairs={{0,16},{16,32},{32,48},{48,64},{64,80},{80,96},{96,112},{112,128},... | collective-permute-start | bytes 1572872 | tf_op jit(solution)/shard_map/ppermute | solution.py:20
  149.6 11.4 %collective-permute-start.4 = (bf16[128,2048]{1,0:T(8,128)(2,1)S(1)}, bf16[128,2048]{1,0:T(8,128)(2,1)S(1)}, u32[]{:S(2)}, u32[]{:S(2)}) collective-permute-start(bf16[128,2048]{1,0:T(8,128)(2,1)S(1)} %combine.3), channel_id=1, source_target_pairs={{0,16},{16,32},{32,48},{48,64},{64,80},{80,96},{96,112},{112,128},... | collective-permute-start | bytes 1572872 | tf_op jit(solution)/shard_map/ppermute | solution.py:20
